TPU v7x, 256 devices: a whole 4x4x8 slice. The times are simulated.
256 devices in a mesh: row: 32 (over x, z), col: 8 (over y, core).
Axes of the slice: x: 4, y: 4, z: 8, core: 2. Of those that a mesh axis runs over, the one named last changes fastest.
Arguments:
- points: float32 [8, 32768], P(None, ('row', 'col')), may hold values from -6 to 6
- length_scales: float32 [8], replicated, may hold values from 1 to 3
- noise: float32 [], replicated, may hold values from 0.5 to 2
- tile_table: int32 [1024], P(('row', 'col')), may hold values from -1 to 31, as said below
- solution: float32 [4, 32768], P(None, ('row', 'col')), may hold values from -6 to 6
- residual: float32 [4, 32768], P(None, ('row', 'col')), may hold values from -6 to 6
- direction: float32 [4, 32768], P(None, ('row', 'col')), may hold values from -6 to 6
Outputs:
- new_solution: float32 [4, 32768], P(None, ('row', 'col'))
- new_residual: float32 [4, 32768], P(None, ('row', 'col'))
- new_direction: float32 [4, 32768], P(None, ('row', 'col'))
Inputs may be any that keep to these rules, and one draw needn't show every extreme that they name: `tile_table`: each entry is -1 or a block index above the row block of its device; every pair of blocks appears at most once; some device of row block 0 has all 4 slots filled, and row block 0 lists block 31.
All inputs are finite; a program needn't handle non-finite values.
Results may differ from a plain program's by a relative error of at most 0.0003.
Values sent between devices are 32-bit elements; how exact they have to be, the bound alone decides.
A program may use at most 64 MiB of HBM per device.

v0:
```python
import math

import jax
import jax.numpy as jnp
from jax import lax
from jax.sharding import PartitionSpec as P

root_five = math.sqrt(5.0)


def kernel_tile(left, right, scales):
    first = left / scales[:, None]
    second = right / scales[:, None]
    cross = lax.dot_general(
        first, second, (((0,), (0,)), ((), ())), precision=lax.Precision.HIGHEST
    )
    dist_sq = (
        jnp.sum(first * first, 0)[:, None] + jnp.sum(second * second, 0)[None, :] - 2.0 * cross
    )
    scaled = root_five * jnp.sqrt(jnp.maximum(dist_sq, 0.0))
    return (1.0 + scaled + scaled * scaled / 3.0) * jnp.exp(-scaled)


def times_kernel(vectors, tile):
    return lax.dot_general(vectors, tile, (((1,), (1,)), ((), ())), precision=lax.Precision.HIGHEST)


def times_kernel_left(vectors, tile):
    return lax.dot_general(vectors, tile, (((1,), (0,)), ((), ())), precision=lax.Precision.HIGHEST)


def local(points, length_scales, noise, tile_table, solution, residual, direction):
    per_device = points.shape[1]
    n_row = lax.axis_size("row")
    n_col = lax.axis_size("col")
    block = per_device * n_col
    all_points, all_dirs = (
        lax.all_gather(points, ("row", "col"), axis=1, tiled=True),
        lax.all_gather(direction, ("row", "col"), axis=1, tiled=True),
    )
    table_full = lax.all_gather(tile_table, ("row", "col"), axis=0, tiled=True)
    row_id = lax.axis_index("row")
    block_ids = jnp.arange(n_row, dtype=jnp.int32)
    table = table_full.reshape(n_row, -1)
    listed = jnp.any(table[:, :, None] == block_ids[None, None, :], axis=1).astype(jnp.float32)
    linked = listed + listed.T
    my_links = lax.dynamic_slice_in_dim(linked, row_id, 1, 0)[0]
    own_start = row_id * block
    own_points = lax.dynamic_slice_in_dim(all_points, own_start, block, 1)
    own_dirs = lax.dynamic_slice_in_dim(all_dirs, own_start, block, 1)

    def add_tile(products, partner):
        far_start = partner * block
        far_points = lax.dynamic_slice_in_dim(all_points, far_start, block, 1)
        far_dirs = lax.dynamic_slice_in_dim(all_dirs, far_start, block, 1)
        tile = kernel_tile(own_points, far_points, length_scales)
        to_own = times_kernel(far_dirs, tile)
        to_far = times_kernel_left(own_dirs, tile)
        current = lax.dynamic_slice_in_dim(products, far_start, block, 1)
        products = lax.dynamic_update_slice_in_dim(products, current + to_far, far_start, 1)
        current = lax.dynamic_slice_in_dim(products, own_start, block, 1)
        return lax.dynamic_update_slice_in_dim(products, current + to_own, own_start, 1)

    def maybe_tile(products, partner, valid):
        return lax.cond(valid, lambda held: add_tile(held, partner), lambda held: held, products)

    diag_weight = 1.0 + jnp.sum(my_links)
    diag_tile = kernel_tile(points, own_points, length_scales)
    diag_term = times_kernel(own_dirs, diag_tile) * diag_weight
    products = jnp.zeros((all_dirs.shape[0], n_row * block), jnp.float32)
    for slot in range(tile_table.shape[0]):
        partner = tile_table[slot]
        products = maybe_tile(products, jnp.maximum(partner, 0), partner >= 0)
    summed = lax.psum_scatter(products, ("row", "col"), scatter_dimension=1, tiled=True)
    image = summed + diag_term + noise * direction
    norm_old = lax.psum(jnp.sum(residual * residual, 1), ("row", "col"))
    curv = lax.psum(jnp.sum(direction * image, 1), ("row", "col"))
    alpha = norm_old / curv
    new_residual = residual - alpha[:, None] * image
    norm_new = lax.psum(jnp.sum(new_residual * new_residual, 1), ("row", "col"))
    new_solution = solution + alpha[:, None] * direction
    new_direction = new_residual + (norm_new / norm_old)[:, None] * direction
    return (new_solution, new_residual, new_direction)


def solution(mesh):
    placed = (
        P(None, ("row", "col")),
        P(),
        P(),
        P(("row", "col")),
        P(None, ("row", "col")),
        P(None, ("row", "col")),
        P(None, ("row", "col")),
    )
    return jax.shard_map(
        local,
        mesh=mesh,
        in_specs=placed,
        out_specs=(P(None, ("row", "col")), P(None, ("row", "col")), P(None, ("row", "col"))),
        check_vma=False,
    )
```

profile of v0, /device:TPU:1, one launch (start us, length us, event | category | flops | bytes accessed | tf_op | source)
XLA Modules:
  0.0 1662.6 jit_solution(15431630383789847384)
XLA Ops:
  7.2 0.7 all-gather.2.cloned.1.call-update
  8.0 1.4 fusion.38
  12.0 73.1 %all_gather.10 = f32[4,32768]{1,0:T(4,128)S(1)} all-gather(f32[4,128]{1,0:T(4,128)} %param.21), channel_id=1, replica_groups=mesh['row'=32,'col'=8] {'row','col'}, dimensions={1}, use_global_device_ids=true | all-gather | bytes 526336 | tf_op jit(solution)/shard_map/all_gather | solution.py:39
  85.1 32.9 %all-gather.2.cloned.1.call-done = f32[8,32768]{1,0:T(8,128)} async-done(((f32[8,128]{1,0:T(8,128)}), f32[8,32768]{1,0:T(8,128)}) %all-gather.2.cloned.1.call-update) | async-done | bytes 1048592 | tf_op jit(solution)/shard_map/all_gather | solution.py:38
  118.0 0.9 multiply_reduce_fusion.8
  118.9 20.6 %conditional.4 = (f32[4,32768]{1,0:T(4,128)}) conditional(s32[]{:T(128)} %bitcast.10, () %tuple.32, (f32[8]{0:T(128)}, f32[8,1024]{1,0:T(8,128)S(1)}, s32[1]{0:T(128)}, f32[8,32768]{1,0:T(8,128)}, f32[4,1024]{1,0:T(4,128)S(1)}, /*index=5*/s32[]{:T(128)}, f32[4,32768]{1,0:T(4,128)S(1)}, s32[1]{0:T(128)}) %tuple.33), branch_computations={%region_2.0_spmd, %region_3.6_spmd} | conditional | flops 212928512 | bytes 30147772 | solution.py:65
  119.5 0.9 multiply_reduce_fusion.1
  120.4 7.0 exponential_multiply_fusion
  127.4 0.9 broadcast_in_dim.2
  128.3 1.1 copy-done
  129.4 2.9 fusion
  132.3 5.7 convolution_add_fusion
  138.0 1.4 dynamic_update_slice.17
  139.4 21.3 %conditional.5 = (f32[4,32768]{1,0:T(4,128)}) conditional(s32[]{:T(128)} %bitcast.9, f32[4,32768]{1,0:T(4,128)} %get-tuple-element.146, (s32[1]{0:T(128)}, f32[4,32768]{1,0:T(4,128)}, f32[8]{0:T(128)}, f32[8,1024]{1,0:T(8,128)S(1)}, f32[8,32768]{1,0:T(8,128)}, /*index=5*/f32[4,1024]{1,0:T(4,128)S(1)}, s32[]{:T(128)}, f32[4,32768]{1,0:T(4,128)S(1)}, ...), branch_computations={%region_6.7_spmd, %region_7.10_spmd} | conditional | flops 212932608 | bytes 29639864 | solution.py:65
  140.2 0.9 multiply_reduce_fusion.3
  141.1 7.0 exponential_multiply_fusion.1
  148.1 1.9 copy-done.1
  150.0 3.6 fusion.5
  153.6 5.7 convolution_add_fusion.1
  159.3 1.4 dynamic_update_slice.19
  160.7 21.3 %conditional.6 = (f32[4,32768]{1,0:T(4,128)}) conditional(s32[]{:T(128)} %bitcast.8, f32[4,32768]{1,0:T(4,128)} %get-tuple-element.147, (s32[1]{0:T(128)}, f32[4,32768]{1,0:T(4,128)}, f32[8]{0:T(128)}, f32[8,1024]{1,0:T(8,128)S(1)}, f32[8,32768]{1,0:T(8,128)}, /*index=5*/f32[4,1024]{1,0:T(4,128)S(1)}, s32[]{:T(128)}, f32[4,32768]{1,0:T(4,128)S(1)}, ...), branch_computations={%region_10.11_spmd, %region_11.14_spmd} | conditional | flops 212932608 | bytes 29639864 | solution.py:65
  161.6 0.9 multiply_reduce_fusion.5
  162.4 7.0 exponential_multiply_fusion.2
  169.4 1.9 copy-done.2
  171.3 3.6 fusion.10
  174.9 5.7 convolution_add_fusion.2
  180.6 1.4 dynamic_update_slice.21
  182.0 21.5 %conditional.7 = (f32[4,32768]{1,0:T(4,128)}) conditional(s32[]{:T(128)} %convert_element_type.30, f32[4,32768]{1,0:T(4,128)} %get-tuple-element.148, (s32[]{:T(128)}, f32[4,32768]{1,0:T(4,128)}, f32[8]{0:T(128)}, f32[8,1024]{1,0:T(8,128)S(1)}, f32[8,32768]{1,0:T(8,128)}, /*index=5*/f32[4,1024]{1,0:T(4,128)S(1)}, s32[]{:T(128)}, ...), branch_computations={%region_14.15_spmd, %region_15.18_spmd} | conditional | flops 212932608 | bytes 29639864 | solution.py:65
  183.1 0.9 multiply_reduce_fusion.7
  183.9 7.0 exponential_multiply_fusion.3
  190.9 1.9 copy-done.3
  192.8 3.6 fusion.15
  196.4 5.7 convolution_add_fusion.3
  202.1 1.4 dynamic_update_slice.23
  203.5 9.1 copy.14
  212.7 0.6 copy-done.9
  213.3 0.2 dynamic-update-slice
  213.4 74.4 %all-reduce = s32[1024]{0:T(1024)S(1)} all-reduce(s32[1024]{0:T(1024)S(1)} %dynamic-update-slice), channel_id=1, replica_groups=mesh['row'=32,'col'=8] {'row','col'}, use_global_device_ids=true, to_apply=%add | all-reduce | flops 1024 | bytes 8192
  287.9 0.2 fusion.32
  288.9 0.7 fusion.35
  290.5 0.9 fusion.22
  291.3 1209.0 %reduce-scatter.4.cloned.1.call-done = f32[128,4]{1,0:T(8,128)} async-done(((f32[32768,4]{1,0:T(8,128)}), f32[128,4]{1,0:T(8,128)}) %reduce-scatter.4.cloned.1.call-update) | async-done | bytes 2064
  1500.3 0.9 copy.15
  1501.2 0.7 multiply_reduce_fusion.11
  1501.9 78.2 %all-reduce.1 = (f32[4]{0:T(128)S(1)}, f32[4]{0:T(128)S(1)}) all-reduce(f32[4]{0:T(128)S(1)} %multiply_reduce_fusion.12, f32[4]{0:T(128)S(1)} %get-tuple-element.144), channel_id=1, replica_groups=mesh['row'=32,'col'=8] {'row','col'}, use_global_device_ids=true, to_apply=%region_1.0 | all-reduce | flops 8 | bytes 64 | tf_op jit(solution)/shard_map/psum | solution.py:76
  1580.2 0.2 multiply_reduce_fusion.10
  1580.4 74.5 %psum.23 = f32[4]{0:T(128)S(1)} all-reduce(f32[4]{0:T(128)S(1)} %get-tuple-element.132), channel_id=1, replica_groups=mesh['row'=32,'col'=8] {'row','col'}, use_global_device_ids=true, to_apply=%region_26.0 | all-reduce | flops 4 | bytes 32 | tf_op jit(solution)/shard_map/psum | solution.py:80
  1654.9 0.7 multiply_add_fusion
  (30 shorter events, 0.5 us)
Async XLA Ops:
  7.2 110.8 %all-gather.2.cloned.1.call-start = ((), (), s32[]{:S(2)}) async-start(), calls=%async_computation.1 | async-start | bytes 1052672 | tf_op jit(solution)/shard_map/all_gather | solution.py:38
  7.9 1492.5 %reduce-scatter.4.cloned.1.call-start = ((), (), s32[]{:S(2)}) async-start(), calls=%async_computation.2 | async-start | bytes 16842752
  127.4 2.1 copy-start
  148.1 1.9 copy-start.1
  169.4 1.9 copy-start.2
  190.9 1.9 copy-start.3
  212.6 0.7 copy-start.9
  212.6 77.6 %copy-start.7 = (f32[4,128]{1,0:T(4,128)S(1)}, f32[4,128]{1,0:T(4,128)}, u32[]{:S(2)}) copy-start(f32[4,128]{1,0:T(4,128)} %param.20) | copy-start | bytes 6148
  212.6 77.8 %copy-start.4 = (f32[8]{0:T(128)S(1)}, f32[8]{0:T(128)}, u32[]{:S(2)}) copy-start(f32[8]{0:T(128)} %param.16) | copy-start | bytes 100
  212.6 77.8 %copy-start.5 = (f32[8,128]{1,0:T(8,128)S(1)}, f32[8,128]{1,0:T(8,128)}, u32[]{:S(2)}) copy-start(f32[8,128]{1,0:T(8,128)} %param.15) | copy-start | bytes 12292
  212.6 1288.6 %copy-start.6 = (f32[4,128]{1,0:T(4,128)S(1)}, f32[4,128]{1,0:T(4,128)}, u32[]{:S(2)}) copy-start(f32[4,128]{1,0:T(4,128)} %param.21) | copy-start | bytes 6148
  212.6 1442.3 %copy-start.10 = (f32[4,128]{1,0:T(4,128)S(1)}, f32[4,128]{1,0:T(4,128)}, u32[]{:S(2)}) copy-start(f32[4,128]{1,0:T(4,128)} %param.19) | copy-start | bytes 6148
  1580.4 75.2 %copy-start.8 = (f32[4,128]{1,0:T(4,128)}, f32[4,128]{1,0:T(4,128)S(1)}, u32[]{:S(2)}) copy-start(f32[4,128]{1,0:T(4,128)S(1)} %get-tuple-element.133) | copy-start | bytes 6148
Sparse Core Ops, SparseCore 0:
  11.7 106.2 all-gather.1
  212.8 1287.5 reduce-scatter.3
where the time goes:
time: 1670 us; the launch traced here: 1660 us
  waiting for transfers between devices  1240 us (74%)
  blocking collectives  300 us (18%)
  matrix products  65.7 us (4%)
  local copies, waits for them, and re-layouts  25.9 us (2%)
  between operations  18.2 us (1%)
    unnamed x3, waiting for transfers between devices  1210 us
    psum x1, blocking collectives, local(): norm_old = lax.psum(jnp.sum(residual * residual, 1), ('row', 'col'))  78.2 us
    psum x1, blocking collectives, local(): norm_new = lax.psum(jnp.sum(new_residual * new_residual, 1), ('row', 'col'))  74.5 us
    unnamed x1, blocking collectives  74.4 us
    all_gather x1, blocking collectives, local(): lax.all_gather(direction, ('row', 'col'), axis=1, tiled=True)  73.1 us
  transfers between devices with their start and end apart: 2, of which 2 were waited for; matrix products, arithmetic and copies ran while one was open for 0% of the time, Pallas kernels for 0%

commit v1 on v0

v1 whole, which is shorter than its diff:
```python
import math

import jax
import jax.numpy as jnp
from jax import lax
from jax.experimental import pallas as pl
from jax.experimental.pallas import tpu as pltpu
from jax.sharding import PartitionSpec as P

F32, BF16 = jnp.float32, jnp.bfloat16
MESH = pl.DeviceIdType.MESH
ROOT3 = math.sqrt(3.0)
RATE = -ROOT3 * math.log2(math.e)
POINT_SCALE = math.sqrt(5.0 / 3.0)
NX, NY, NZ, NC = 4, 4, 8, 2
GROUP = 16
W = 128
DEPTH = 64


def split3(a):
    high = a.astype(BF16).astype(F32)
    rest = a - high
    mid = rest.astype(BF16).astype(F32)
    return high, mid, rest - mid


def norm_rows(a, first):
    n = split3(jnp.sum(a * a, axis=0, keepdims=True))
    row = lax.broadcasted_iota(jnp.int32, a.shape, 0)
    at = 0 if first else 3
    ones = ((row >= 3 - at) & (row < 6 - at)).astype(F32)
    for k in range(3):
        ones = jnp.where(row == at + k, n[k], ones)
    return ones


def right_rows(a):
    h, m, l = split3(a)
    return jnp.concatenate([h, h, h, m, m, l, norm_rows(a, False), jnp.zeros_like(a)], 0)


def left_rows(a):
    h, m, l = (-2.0 * part for part in split3(a))
    return jnp.concatenate([h, m, l, h, m, h, norm_rows(a, True), jnp.zeros_like(a)], 0)


def kern_of(s):
    s = jnp.maximum(s, 1e-30)
    v = s * lax.rsqrt(s)
    return ((v + ROOT3) * v + 1.0) * jnp.exp2(v * RATE)


def body(
    scales, noise, table, points, sol, res, dirs, new_sol, new_res, new_dir,
    pbuf, qbuf, tbuf, rbuf, s1buf, s2buf, sendr, left, right, dlhs, acc, wbuf,
    p_recv, q_recv, t_recv, r_recv, s1_recv, s2_recv, send_sem,
):
    row, col = lax.axis_index("row"), lax.axis_index("col")
    x, z = lax.div(row, NZ), lax.rem(row, NZ)
    y, core = lax.div(col, NC), lax.rem(col, NC)

    def p_at(k, sign):
        zz = lax.rem(z + (sign * (k % NZ)) % NZ, NZ)
        cc = lax.rem(core + k // NZ, NC)
        return (x * NZ + zz, y * NC + cc)

    def q_at(m, sign):
        xx = lax.rem(x + (sign * (m // NY)) % NX, NX)
        yy = lax.rem(y + (sign * (m % NY)) % NY, NY)
        return (xx * NZ + z, yy * NC + core)

    others = range(1, GROUP)
    barrier = pltpu.get_barrier_semaphore()
    for k in others:
        pl.semaphore_signal(barrier, inc=1, device_id=p_at(k, 1), device_id_type=MESH)
        pl.semaphore_signal(barrier, inc=1, device_id=q_at(k, 1), device_id_type=MESH)

    sub = lax.broadcasted_iota(jnp.int32, (8, W), 0)
    lane = lax.broadcasted_iota(jnp.int32, (8, W), 1)
    col_scale = jnp.full((8, W), scales[0], F32)
    for f in range(1, 8):
        col_scale = jnp.where(sub == f, scales[f], col_scale)
    a = points[...] / col_scale * POINT_SCALE
    pbuf[0] = a
    lane1 = lax.broadcasted_iota(jnp.int32, (1, W), 1)
    own_table = jnp.full((1, W), table[0].astype(F32), F32)
    for s in range(1, 4):
        own_table = jnp.where(lax.rem(lane1, 4) == s, table[s].astype(F32), own_table)
    qbuf[0, 0:8] = a
    qbuf[0, 8:12] = dirs[...]
    qbuf[0, 12:16] = jnp.broadcast_to(own_table, (4, W))

    def p_copy(src, buf, recv, k, sem, sign=1):
        return pltpu.make_async_remote_copy(
            src_ref=src, dst_ref=buf.at[k], send_sem=send_sem.at[sem, k], recv_sem=recv.at[k],
            device_id=p_at(k, sign), device_id_type=MESH,
        )

    def q_copy(src, buf, recv, k, sem):
        return pltpu.make_async_remote_copy(
            src_ref=src, dst_ref=buf.at[k], send_sem=send_sem.at[sem, k], recv_sem=recv.at[k],
            device_id=q_at(k, 1), device_id_type=MESH,
        )

    pl.semaphore_wait(barrier, 2 * (GROUP - 1))
    p_copies = {k: p_copy(pbuf.at[0], pbuf, p_recv, k, 0) for k in others}
    q_copies = {k: q_copy(qbuf.at[0], qbuf, q_recv, k, 1) for k in others}
    for k in others:
        p_copies[k].start()
        q_copies[k].start()

    def prep_right(k):
        right[:, pl.ds(k * W, W)] = right_rows(pbuf[k]).astype(BF16)

    def prep_left(m):
        left[pl.ds(m * W, W), :] = left_rows(qbuf[m, 0:8]).T.astype(BF16)
        h, mid, low = split3(qbuf[m, 8:12])
        dlhs[:, pl.ds(m * W, W)] = jnp.concatenate([h, mid, low, jnp.zeros_like(h)], 0).astype(BF16)

    def tile(pair, mx, first, ppair):
        q0, p0 = pair * 256, ppair * 256
        s = jnp.dot(left[pl.ds(q0, 256), :], right[:, pl.ds(p0, 256)], preferred_element_type=F32)
        kern = kern_of(s)
        high = kern.astype(BF16)
        low = (kern - high.astype(F32)).astype(BF16)
        d = dlhs[:, pl.ds(q0, 256)]
        both = jnp.dot(d, high, preferred_element_type=F32)
        both += jnp.dot(d, low, preferred_element_type=F32)
        at = (mx, slice(None), pl.ds(p0, 256))
        acc[at] = both if first else acc[at] + both

    prep_right(0)
    prep_left(0)
    for k in others:
        p_copies[k].wait_recv()
        prep_right(k)
    for pair in range(8):
        for m in (2 * pair, 2 * pair + 1):
            if m > 0:
                q_copies[m].wait_recv()
                prep_left(m)
        for ppair in range(8):
            tile(pair, pair // 2, pair % 2 == 0, ppair)

    joined = jnp.where(lane1 < 4, qbuf[0, 12:13], -1.0)
    for m in others:
        joined = jnp.where(lax.div(lane1, 4) == m, qbuf[m, 12:13], joined)
    tbuf[0] = joined
    t_copies = {k: p_copy(tbuf.at[0], tbuf, t_recv, k, 2) for k in others}
    for k in others:
        t_copies[k].start()
    for k in others:
        t_copies[k].wait_recv()

    tt = [jnp.concatenate([tbuf[kc * NZ + kz] for kz in range(NZ)], 0) for kc in range(NC)]
    rp = (x * NZ + lax.rem(z + NZ - sub, NZ)).astype(F32)
    own = row.astype(F32)
    far = sum((jnp.broadcast_to(t[0:1], (8, W)) == rp).astype(F32) for t in tt)
    degree = sum(
        jnp.where((t == own) | ((t >= 0.0) & (lane < 16) & (sub == 0)), 1.0, 0.0) for t in tt
    )
    degree = jnp.sum(jnp.sum(degree, axis=1, keepdims=True), axis=0, keepdims=True)
    for mx in range(NX):
        rq = (lax.rem(x + NX - mx, NX) * NZ + z).astype(F32)
        listed = jnp.where(lax.div(lane, 16) == mx, far, 0.0)
        listed += sum(((t == rq) & (lane < 16)).astype(F32) for t in tt)
        weight = jnp.broadcast_to(jnp.sum(listed, axis=1, keepdims=True), (8, W))
        if mx == 0:
            weight = jnp.where(sub == 0, 1.0 + degree, weight)
        wbuf[mx] = weight

    def partial(k):
        total = jnp.zeros((4, W), F32)
        for mx in range(NX):
            at = pl.ds(k * W, W)
            part = acc[mx, 0:4, at] + (acc[mx, 4:8, at] + acc[mx, 8:12, at])
            total += part * wbuf[mx, pl.ds(k % NZ, 1), :]
        return total

    r_copies = {k: p_copy(sendr.at[k], rbuf, r_recv, k, 3, -1) for k in others}
    for k in others:
        sendr[k] = partial(k)
        r_copies[k].start()
    d = dirs[...]
    image = partial(0) + noise[0] * d
    for k in others:
        r_copies[k].wait_recv()
        image += rbuf[k]

    r = res[...]
    parts = jnp.concatenate([r * r, d * image, r * image, image * image], 0)
    sums = jnp.sum(parts, axis=1, keepdims=True)
    sub16 = lax.broadcasted_iota(jnp.int32, (16, W), 0)
    lane16 = lax.broadcasted_iota(jnp.int32, (16, W), 1)

    s1buf[0] = jnp.sum(jnp.where(sub16 == lane16, sums, 0.0), axis=0, keepdims=True)
    s1_copies = {k: p_copy(s1buf.at[0], s1buf, s1_recv, k, 4) for k in others}
    for k in others:
        s1_copies[k].start()
    for k in others:
        s1_copies[k].wait_recv()
    s2buf[0] = jnp.sum(s1buf[...], axis=0)
    s2_copies = {k: q_copy(s2buf.at[0], s2buf, s2_recv, k, 5) for k in others}
    for k in others:
        s2_copies[k].start()
    for k in others:
        s2_copies[k].wait_recv()
    total = jnp.sum(s2buf[...], axis=0)
    sums = jnp.sum(jnp.where(sub16 == lane16, total, 0.0), axis=1, keepdims=True)
    rr, curv, ri, ii = (sums[4 * i : 4 * i + 4] for i in range(4))
    alpha = rr / curv
    rr_new = jnp.maximum(rr - alpha * (2.0 * ri - alpha * ii), 0.0)
    beta = rr_new / rr
    nr = r - alpha * image
    new_sol[...] = sol[...] + alpha * d
    new_res[...] = nr
    new_dir[...] = nr + beta * d
    for copies in (p_copies, q_copies, t_copies, r_copies, s1_copies, s2_copies):
        for k in others:
            copies[k].wait_send()


def local(points, length_scales, noise, tile_table, solution, residual, direction):
    vmem = pl.BlockSpec(memory_space=pltpu.VMEM)
    smem = pl.BlockSpec(memory_space=pltpu.SMEM)
    out = jax.ShapeDtypeStruct(direction.shape, F32)
    dma = pltpu.SemaphoreType.DMA
    return pl.pallas_call(
        body,
        out_shape=(out, out, out),
        in_specs=[smem, smem, smem, vmem, vmem, vmem, vmem],
        out_specs=(vmem, vmem, vmem),
        scratch_shapes=[
            pltpu.VMEM((GROUP, 8, W), F32),
            pltpu.VMEM((GROUP, 16, W), F32),
            pltpu.VMEM((GROUP, 1, W), F32),
            pltpu.VMEM((GROUP, 4, W), F32),
            pltpu.VMEM((GROUP, 1, W), F32),
            pltpu.VMEM((GROUP, 1, W), F32),
            pltpu.VMEM((GROUP, 4, W), F32),
            pltpu.VMEM((GROUP * W, DEPTH), BF16),
            pltpu.VMEM((DEPTH, GROUP * W), BF16),
            pltpu.VMEM((16, GROUP * W), BF16),
            pltpu.VMEM((NX, 16, GROUP * W), F32),
            pltpu.VMEM((NX, 8, W), F32),
        ]
        + [dma((GROUP,))] * 6
        + [dma((6, GROUP))],
        compiler_params=pltpu.CompilerParams(
            collective_id=0, has_side_effects=True, vmem_limit_bytes=40 * 2**20
        ),
    )(length_scales, noise.reshape(1), tile_table, points, solution, residual, direction)


def solution(mesh):
    vec = P(None, ("row", "col"))
    return jax.shard_map(
        local,
        mesh=mesh,
        in_specs=(vec, P(), P(), P(("row", "col")), vec, vec, vec),
        out_specs=(vec, vec, vec),
        check_vma=False,
    )
```

time: 1670 us -> 52.5 us (0.03)
  waiting for transfers between devices: 1240 us -> 0 us
  blocking collectives: 300 us -> 0 us
  matrix products: 65.7 us -> 0 us
  Pallas kernels: 0 us -> 46.5 us
  local copies, waits for them, and re-layouts: 25.9 us -> 4.43 us
  between operations: 18.2 us -> 1.34 us
    unnamed x3 -> x0, waiting for transfers between devices: 1210 us -> none
    psum x2 -> x0, blocking collectives: 153 us -> none  [the longest x1 78.2 us: local(): norm_old = lax.psum(jnp.sum(residual * residual, 1), ('row', 'col'))]
    unnamed x1 -> x0, blocking collectives: 74.4 us -> none
    all_gather x1 -> x0, blocking collectives: 73.1 us -> none  [local(): lax.all_gather(direction, ('row', 'col'), axis=1, tiled=True)]
    dot_general x14 -> x0, matrix products: 65.7 us -> none  [the longest x5 28.7 us: kernel_tile(): lax.dot_general(first, second, (((0,), (0,)), ((), ())), precision=lax.Pr...]
    pallas_call x0 -> x1, Pallas kernels: none -> 46.5 us  [local(): pl.pallas_call(body, out_shape=(out, out, out), in_specs=[smem, smem, sme...]
    all_gather x1 -> x0, waiting for transfers between devices: 32.9 us -> none  [local(): lax.all_gather(points, ('row', 'col'), axis=1, tiled=True)]
  transfers between devices with their start and end apart: 2 -> 0, of which waited for: 2 -> 0; matrix products, arithmetic and copies ran while one was open for 0% -> 0% of each run, Pallas kernels for 0% -> 0%
where the time goes in v1:
time: 52.5 us; the launch traced here: 52.3 us
  Pallas kernels  46.5 us (89%)
  local copies, waits for them, and re-layouts  4.43 us (8%)
  between operations  1.34 us (3%)
    pallas_call x1, Pallas kernels, local(): pl.pallas_call(body, out_shape=(out, out, out), in_specs=[smem, smem, sme...  46.5 us
    unnamed x15, local copies, waits for them, and re-layouts  4.43 us

profile of v1, /device:TPU:1, one launch (start us, length us, event | category | flops | bytes accessed | tf_op | source)
XLA Modules:
  0.0 52.3 jit_solution(9289873834210946532)
XLA Ops:
  0.6 0.0 copy-start.1
  1.3 0.0 copy-start.4
  1.3 0.0 copy-start.5
  1.3 0.0 copy-done.1
  1.3 0.6 %copy-done.4 = f32[8]{0:T(128)S(1)} copy-done((f32[8]{0:T(128)S(1)}, f32[8]{0:T(128)}, u32[]{:S(2)}) %copy-start.4) | copy-done | bytes 56
  2.0 0.0 copy-done.5
  2.0 0.0 copy-start
  2.0 0.7 %copy-done = f32[8,128]{1,0:T(8,128)S(1)} copy-done((f32[8,128]{1,0:T(8,128)S(1)}, f32[8,128]{1,0:T(8,128)}, u32[]{:S(2)}) %copy-start) | copy-done | bytes 4120
  2.7 0.0 copy-start.2
  2.7 0.7 %copy-done.2 = f32[4,128]{1,0:T(4,128)S(1)} copy-done((f32[4,128]{1,0:T(4,128)S(1)}, f32[4,128]{1,0:T(4,128)}, u32[]{:S(2)}) %copy-start.2) | copy-done | bytes 2072
  3.3 0.0 copy-start.3
  3.3 0.7 %copy-done.3 = f32[4,128]{1,0:T(4,128)S(1)} copy-done((f32[4,128]{1,0:T(4,128)S(1)}, f32[4,128]{1,0:T(4,128)}, u32[]{:S(2)}) %copy-start.3) | copy-done | bytes 2072
  4.0 46.5 %shard_map.94 = (f32[4,128]{1,0:T(4,128)S(1)}, f32[4,128]{1,0:T(4,128)S(1)}, f32[4,128]{1,0:T(4,128)S(1)}) custom-call(f32[8]{0:T(128)S(1)} %copy-done.4, f32[1]{0:T(128)} %bitcast.1.noise, s32[4]{0:T(128)S(1)} %copy-done.5, f32[8,128]{1,0:T(8,128)S(1)} %copy-done, f32[4,128]{1,0:T(4,128)S(1)} %copy-done.1, f32[4,128]{1,0:T(4,128)S(1)} %copy-done.2, ...), custom_call_target="tpu_custom_call" | custom-call | tf_op jit(solution)/shard_map/pallas_call | solution.py:229
  50.5 0.6 %copy.14 = f32[4,128]{1,0:T(4,128)} copy(f32[4,128]{1,0:T(4,128)S(1)} %get-tuple-element.6) | data formatting | bytes 4096
  51.1 0.6 %copy.15 = f32[4,128]{1,0:T(4,128)} copy(f32[4,128]{1,0:T(4,128)S(1)} %get-tuple-element.7) | data formatting | bytes 4096
  51.7 0.6 %copy.16 = f32[4,128]{1,0:T(4,128)} copy(f32[4,128]{1,0:T(4,128)S(1)} %get-tuple-element.8) | data formatting | bytes 4096
Async XLA Ops:
  0.6 0.7 %copy-start.1 = (f32[4,128]{1,0:T(4,128)S(1)}, f32[4,128]{1,0:T(4,128)}, u32[]{:S(2)}) copy-start(f32[4,128]{1,0:T(4,128)} %sol.1) | copy-start | bytes 6148
  1.3 0.7 %copy-start.4 = (f32[8]{0:T(128)S(1)}, f32[8]{0:T(128)}, u32[]{:S(2)}) copy-start(f32[8]{0:T(128)} %scales.1) | copy-start | bytes 100
  1.3 0.7 %copy-start.5 = (s32[4]{0:T(128)S(1)}, s32[4]{0:T(128)}, u32[]{:S(2)}) copy-start(s32[4]{0:T(128)} %table.1) | copy-start | bytes 52
  2.0 0.7 %copy-start = (f32[8,128]{1,0:T(8,128)S(1)}, f32[8,128]{1,0:T(8,128)}, u32[]{:S(2)}) copy-start(f32[8,128]{1,0:T(8,128)} %points.1) | copy-start | bytes 12292
  2.7 0.7 %copy-start.2 = (f32[4,128]{1,0:T(4,128)S(1)}, f32[4,128]{1,0:T(4,128)}, u32[]{:S(2)}) copy-start(f32[4,128]{1,0:T(4,128)} %res.1) | copy-start | bytes 6148
  3.3 0.7 %copy-start.3 = (f32[4,128]{1,0:T(4,128)S(1)}, f32[4,128]{1,0:T(4,128)}, u32[]{:S(2)}) copy-start(f32[4,128]{1,0:T(4,128)} %dirs.1) | copy-start | bytes 6148

commit v2 on v1

v2 whole, which is shorter than its diff:
```python
import math

import jax
import jax.numpy as jnp
from jax import lax
from jax.experimental import pallas as pl
from jax.experimental.pallas import tpu as pltpu
from jax.sharding import PartitionSpec as P

F32, BF16 = jnp.float32, jnp.bfloat16
MESH = pl.DeviceIdType.MESH
ROOT3 = math.sqrt(3.0)
RATE = -ROOT3 * math.log2(math.e)
POINT_SCALE = math.sqrt(5.0 / 3.0)
NX, NY, NZ, NC = 4, 4, 8, 2
CHIPS = NX * NY * NZ
GROUP = 16
W = 128
DEPTH = 64


def split3(a):
    high = a.astype(BF16).astype(F32)
    rest = a - high
    mid = rest.astype(BF16).astype(F32)
    return high, mid, rest - mid


def norm_rows(a, first):
    n = split3(jnp.sum(a * a, axis=0, keepdims=True))
    row = lax.broadcasted_iota(jnp.int32, a.shape, 0)
    at = 0 if first else 3
    ones = ((row >= 3 - at) & (row < 6 - at)).astype(F32)
    for k in range(3):
        ones = jnp.where(row == at + k, n[k], ones)
    return ones


def right_rows(a):
    h, m, l = split3(a)
    return jnp.concatenate([h, h, h, m, m, l, norm_rows(a, False), jnp.zeros_like(a)], 0)


def left_rows(a):
    h, m, l = (-2.0 * part for part in split3(a))
    return jnp.concatenate([h, m, l, h, m, h, norm_rows(a, True), jnp.zeros_like(a)], 0)


def kern_of(s):
    s = jnp.maximum(s, 1e-30)
    v = s * lax.rsqrt(s)
    return ((v + ROOT3) * v + 1.0) * jnp.exp2(v * RATE)


def body(
    scales_in, noise_in, table_in, points_in, sol_in, res_in, dirs_in, out,
    scales, noise, table, points, sol, res, dirs,
    pbuf, qbuf, tbuf, rbuf, s1buf, s2buf, sendr, left, right, dlhs, acc,
    in_sem, p_recv, q_recv, t_recv, r_recv, s1_recv, s2_recv, send_sem,
):
    row, col = lax.axis_index("row"), lax.axis_index("col")
    x, z = lax.div(row, NZ), lax.rem(row, NZ)
    y, core = lax.div(col, NC), lax.rem(col, NC)

    def p_at(k, sign):
        zz = lax.rem(z + (sign * (k // NC)) % NZ, NZ)
        cc = lax.rem(core + k % NC, NC)
        return (x * NZ + zz, y * NC + cc)

    def q_at(m, sign):
        xx = lax.rem(x + (sign * (m // NY)) % NX, NX)
        yy = lax.rem(y + (sign * (m % NY)) % NY, NY)
        return (xx * NZ + z, yy * NC + core)

    loads = [
        pltpu.make_async_copy(src, dst, in_sem.at[i])
        for i, (src, dst) in enumerate(
            (
                (points_in, points), (scales_in, scales), (table_in, table), (dirs_in, dirs),
                (noise_in, noise), (sol_in, sol), (res_in, res),
            )
        )
    ]
    others = range(1, GROUP)
    barrier = pltpu.get_barrier_semaphore()
    for k in others:
        pl.semaphore_signal(barrier, inc=1, device_id=p_at(k, 1), device_id_type=MESH)
        pl.semaphore_signal(barrier, inc=1, device_id=q_at(k, 1), device_id_type=MESH)

    for load in loads:
        load.start()
    sub = lax.broadcasted_iota(jnp.int32, (8, W), 0)
    lane = lax.broadcasted_iota(jnp.int32, (8, W), 1)
    for load in loads[:5]:
        load.wait()
    col_scale = jnp.full((8, W), scales[0], F32)
    for f in range(1, 8):
        col_scale = jnp.where(sub == f, scales[f], col_scale)
    a = points[...] / col_scale * POINT_SCALE
    pbuf[0] = a
    lane1 = lax.broadcasted_iota(jnp.int32, (1, W), 1)
    own_table = jnp.full((1, W), table[0].astype(F32), F32)
    for s in range(1, 4):
        own_table = jnp.where(lax.rem(lane1, 4) == s, table[s].astype(F32), own_table)
    qbuf[0, 0:8] = a
    qbuf[0, 8:12] = dirs[...]
    qbuf[0, 12:16] = jnp.broadcast_to(own_table, (4, W))

    def p_copy(src, buf, recv, k, sem, sign=1):
        return pltpu.make_async_remote_copy(
            src_ref=src, dst_ref=buf.at[k], send_sem=send_sem.at[sem, k], recv_sem=recv.at[k],
            device_id=p_at(k, sign), device_id_type=MESH,
        )

    def q_copy(src, buf, recv, k, sem):
        return pltpu.make_async_remote_copy(
            src_ref=src, dst_ref=buf.at[k], send_sem=send_sem.at[sem, k], recv_sem=recv.at[k],
            device_id=q_at(k, 1), device_id_type=MESH,
        )

    pl.semaphore_wait(barrier, 2 * (GROUP - 1))
    p_copies = {k: p_copy(pbuf.at[0], pbuf, p_recv, k, 0) for k in others}
    q_copies = {k: q_copy(qbuf.at[0], qbuf, q_recv, k, 1) for k in others}
    for k in others:
        p_copies[k].start()
        q_copies[k].start()

    def prep_right(k):
        right[:, pl.ds(k * W, W)] = right_rows(pbuf[k]).astype(BF16)

    def prep_left(m):
        left[pl.ds(m * W, W), :] = left_rows(qbuf[m, 0:8]).T.astype(BF16)
        h, mid, low = split3(qbuf[m, 8:12])
        dlhs[:, pl.ds(m * W, W)] = jnp.concatenate([h, mid, low, jnp.zeros_like(h)], 0).astype(BF16)

    def tile(pair, mx, first, ppair):
        q0, p0 = pair * 256, ppair * 256
        s = jnp.dot(left[pl.ds(q0, 256), :], right[:, pl.ds(p0, 256)], preferred_element_type=F32)
        kern = kern_of(s)
        high = kern.astype(BF16)
        low = (kern - high.astype(F32)).astype(BF16)
        d = dlhs[:, pl.ds(q0, 256)]
        both = jnp.dot(d, high, preferred_element_type=F32)
        both += jnp.dot(d, low, preferred_element_type=F32)
        at = (mx, slice(None), pl.ds(p0, 256))
        acc[at] = both if first else acc[at] + both

    def arrive_p(*pairs):
        for pair in pairs:
            for k in (2 * pair, 2 * pair + 1):
                if k > 0:
                    p_copies[k].wait_recv()
                prep_right(k)

    def arrive_q(*pairs):
        for pair in pairs:
            for m in (2 * pair, 2 * pair + 1):
                if m > 0:
                    q_copies[m].wait_recv()
                prep_left(m)

    def region(step):
        pl.when(row >= 0)(step)

    done = set()

    def tiles(ppairs, pairs):
        for ppair in ppairs:
            for pair in pairs:
                if (ppair, pair) not in done:
                    first = (ppair, pair ^ 1) not in done
                    tile(pair, pair // 2, first, ppair)
                    done.add((ppair, pair))

    @region
    def _():
        arrive_p(0, 1, 7)
        arrive_q(0)
        tiles((0, 1, 7), (0,))

    @region
    def _():
        arrive_q(1, 2, 6)
        tiles((0, 1, 7), (1, 2, 6))

    @region
    def _():
        arrive_p(2, 6)
        tiles((2, 6), (0, 1, 2, 6))

    arrive_p(3, 5, 4)
    arrive_q(3, 7, 4, 5)

    joined = jnp.where(lane1 < 4, qbuf[0, 12:13], -1.0)
    for m in others:
        joined = jnp.where(lax.div(lane1, 4) == m, qbuf[m, 12:13], joined)
    tbuf[0] = joined
    t_copies = {k: p_copy(tbuf.at[0], tbuf, t_recv, k, 2) for k in others}
    for k in others:
        t_copies[k].start()

    r_copies = {k: p_copy(sendr.at[k], rbuf, r_recv, k, 3, -1) for k in others}
    def finish(ppairs):
        tiles(ppairs, range(8))
        for k in (2 * p + kc for p in ppairs for kc in range(NC)):
            for mx in range(NX):
                at = pl.ds(k * W, W)
                sendr[k, 4 * mx : 4 * mx + 4] = acc[mx, 0:4, at] + (
                    acc[mx, 4:8, at] + acc[mx, 8:12, at]
                )
            if k > 0:
                r_copies[k].start()

    region(lambda: finish((4, 3, 5)))
    region(lambda: finish((2, 6)))
    region(lambda: finish((1, 7, 0)))

    for k in others:
        t_copies[k].wait_recv()

    sub16 = lax.broadcasted_iota(jnp.int32, (16, W), 0)
    lane16 = lax.broadcasted_iota(jnp.int32, (16, W), 1)
    group = lax.div(sub16, 4)
    tt = [jnp.concatenate([tbuf[2 * kz + kc] for kz in range(NZ)], 0) for kc in range(NC)]
    own = row.astype(F32)
    lists_me = sum((t == own).astype(F32) for t in tt)
    degree = lists_me + sum(
        jnp.where((t >= 0.0) & (lane < 16) & (sub == 0), 1.0, 0.0) for t in tt
    )
    degree = jnp.sum(jnp.sum(degree, axis=1, keepdims=True), axis=0, keepdims=True)
    mine = [jnp.where(lane1 < 16, t[0:1], -1.0) for t in tt]
    d = dirs[...]
    weighted = jnp.zeros((16, W), F32)
    for kz in (4, 3, 5, 2, 6, 1, 7, 0):
        at = (NZ - kz) % NZ
        block = (lax.rem(x + NX - group, NX) * NZ + lax.rem(z + kz, NZ)).astype(F32)
        linked = jnp.where(lax.div(lane16, 16) == group, lists_me[at : at + 1], 0.0)
        linked += sum((t == block).astype(F32) for t in mine)
        weight = jnp.sum(linked, axis=1, keepdims=True)
        if kz == 0:
            weight = jnp.where(sub16[:, 0:1] < 4, 1.0 + degree, weight)
        for k in (2 * kz, 2 * kz + 1):
            if k > 0:
                r_copies[k].wait_recv()
            weighted += weight * (rbuf[k] if k > 0 else sendr[0])
    image = sum(weighted[4 * mx : 4 * mx + 4] for mx in range(NX)) + noise[0] * d

    loads[5].wait()
    loads[6].wait()
    r = res[...]
    parts = jnp.concatenate([r * r, d * image, r * image, image * image], 0)
    sums = jnp.sum(parts, axis=1, keepdims=True)
    s1buf[0] = jnp.sum(jnp.where(sub16 == lane16, sums, 0.0), axis=0, keepdims=True)
    pair_copy = p_copy(s1buf.at[0], s1buf, s1_recv, 1, 4)
    pair_copy.start()
    pair_copy.wait_recv()
    s2buf[0] = s1buf[0] + s1buf[1]

    xs = [lax.rem(x + d, NX) * NZ for d in range(NX)]
    ys = [lax.rem(y + d, NY) * NC + core for d in range(NY)]
    zs = [lax.rem(z + d, NZ) for d in range(NZ)]

    def hops(slot):
        at = ((slot // 32, NX), (slot // 8 % 4, NY), (slot % 8, NZ))
        return sum(min(d, extent - d) for d, extent in at)

    for slot in sorted(range(1, CHIPS), key=hops, reverse=True):
        pltpu.make_async_remote_copy(
            src_ref=s2buf.at[0], dst_ref=s2buf.at[slot],
            send_sem=send_sem.at[5, 0], recv_sem=s2_recv.at[0],
            device_id=(xs[slot // 32] + zs[slot % 8], ys[slot // 8 % 4]), device_id_type=MESH,
        ).start()
    rest = s2buf.at[pl.ds(1, CHIPS - 1)]
    pltpu.make_async_copy(rest, rest, s2_recv.at[0]).wait()
    total = jnp.sum(s2buf[...], axis=0)
    sums = jnp.sum(jnp.where(sub16 == lane16, total, 0.0), axis=1, keepdims=True)
    rr, curv, ri, ii = (sums[4 * i : 4 * i + 4] for i in range(4))
    alpha = rr / curv
    rr_new = jnp.maximum(rr - alpha * (2.0 * ri - alpha * ii), 0.0)
    beta = rr_new / rr
    nr = r - alpha * image
    out[0:4] = sol[...] + alpha * d
    out[4:8] = nr
    out[8:12] = nr + beta * d
    pair_copy.wait_send()
    pltpu.make_async_copy(rest, rest, send_sem.at[5, 0]).wait()
    for copies in (p_copies, q_copies, t_copies, r_copies):
        for k in others:
            copies[k].wait_send()


def local(points, length_scales, noise, tile_table, solution, residual, direction):
    hbm = pl.BlockSpec(memory_space=pltpu.HBM)
    dma = pltpu.SemaphoreType.DMA
    out = pl.pallas_call(
        body,
        out_shape=jax.ShapeDtypeStruct((12, W), F32),
        in_specs=[hbm] * 7,
        out_specs=pl.BlockSpec(memory_space=pltpu.VMEM),
        scratch_shapes=[
            pltpu.SMEM((8,), F32),
            pltpu.SMEM((1,), F32),
            pltpu.SMEM((4,), jnp.int32),
            pltpu.VMEM((8, W), F32),
            pltpu.VMEM((4, W), F32),
            pltpu.VMEM((4, W), F32),
            pltpu.VMEM((4, W), F32),
            pltpu.VMEM((GROUP, 8, W), F32),
            pltpu.VMEM((GROUP, 16, W), F32),
            pltpu.VMEM((GROUP, 1, W), F32),
            pltpu.VMEM((GROUP, 16, W), F32),
            pltpu.VMEM((2, 1, W), F32),
            pltpu.VMEM((CHIPS, 1, W), F32),
            pltpu.VMEM((GROUP, 16, W), F32),
            pltpu.VMEM((GROUP * W, DEPTH), BF16),
            pltpu.VMEM((DEPTH, GROUP * W), BF16),
            pltpu.VMEM((16, GROUP * W), BF16),
            pltpu.VMEM((NX, 16, GROUP * W), F32),
            dma((7,)),
        ]
        + [dma((GROUP,))] * 6
        + [dma((6, GROUP))],
        compiler_params=pltpu.CompilerParams(
            collective_id=0, has_side_effects=True, vmem_limit_bytes=64 * 2**20 - 65536
        ),
    )(length_scales, noise.reshape(1), tile_table, points, solution, residual, direction)
    return out[0:4], out[4:8], out[8:12]


def solution(mesh):
    vec = P(None, ("row", "col"))
    return jax.shard_map(
        local,
        mesh=mesh,
        in_specs=(vec, P(), P(), P(("row", "col")), vec, vec, vec),
        out_specs=(vec, vec, vec),
        check_vma=False,
    )
```

time: 52.5 us -> 41.3 us (0.79)
  Pallas kernels: 46.5 us -> 38.6 us
  local copies, waits for them, and re-layouts: 4.43 us -> 1.34 us
    pallas_call x1, Pallas kernels: 46.5 us -> 38.6 us  [local(): pl.pallas_call(body, out_shape=jax.ShapeDtypeStruct((12, W), F32), in_spe...]
    unnamed x15 -> x0, local copies, waits for them, and re-layouts: 4.43 us -> none
    slice x0 -> x1, local copies, waits for them, and re-layouts: none -> 1.34 us  [local(): return (out[0:4], out[4:8], out[8:12])]
where the time goes in v2:
time: 41.3 us; the launch traced here: 41.2 us
  Pallas kernels  38.6 us (93%)
  local copies, waits for them, and re-layouts  1.34 us (3%)
  between operations  1.29 us (3%)
    pallas_call x1, Pallas kernels, local(): pl.pallas_call(body, out_shape=jax.ShapeDtypeStruct((12, W), F32), in_spe...  38.6 us
    slice x1, local copies, waits for them, and re-layouts, local(): return (out[0:4], out[4:8], out[8:12])  1.34 us

profile of v2, /device:TPU:1, one launch (start us, length us, event | category | flops | bytes accessed | tf_op | source)
XLA Modules:
  0.0 41.2 jit_solution(315656788745118441)
XLA Ops:
  1.3 38.6 %shard_map.94 = f32[12,128]{1,0:T(8,128)} custom-call(f32[8]{0:T(128)} %scales_in.1, f32[1]{0:T(128)} %bitcast.1.noise_in, s32[4]{0:T(128)} %table_in.1, f32[8,128]{1,0:T(8,128)} %points_in.1, f32[4,128]{1,0:T(4,128)} %sol_in.1, f32[4,128]{1,0:T(4,128)} %res_in.1, f32[4,128]{1,0:T(4,128)} %dirs_in.1), custom_call_target="tpu_custom_call" | custom-call | tf_op jit(solution)/shard_map/pallas_call | solution.py:295
  39.9 1.3 %fusion = (f32[4,128]{1,0:T(4,128)}, f32[4,128]{1,0:T(4,128)}, f32[4,128]{1,0:T(4,128)}) fusion(f32[12,128]{1,0:T(8,128)} %shard_map.94), kind=kLoop, calls=%fused_computation | loop fusion | bytes 12288 | tf_op jit(solution)/shard_map/slice | solution.py:327

commit v3 on v2

--- a/solution.py
+++ b/solution.py
@@ -49,7 +49,7 @@
 def kern_of(s):
     s = jnp.maximum(s, 1e-30)
     v = s * lax.rsqrt(s)
-    return ((v + ROOT3) * v + 1.0) * jnp.exp2(v * RATE)
+    return (s + (ROOT3 * v + 1.0)) * jnp.exp2(v * RATE)
 
 
 def body(
@@ -172,23 +172,12 @@
                     tile(pair, pair // 2, first, ppair)
                     done.add((ppair, pair))
 
-    @region
-    def _():
-        arrive_p(0, 1, 7)
-        arrive_q(0)
-        tiles((0, 1, 7), (0,))
-
-    @region
-    def _():
-        arrive_q(1, 2, 6)
-        tiles((0, 1, 7), (1, 2, 6))
-
-    @region
-    def _():
-        arrive_p(2, 6)
-        tiles((2, 6), (0, 1, 2, 6))
-
-    arrive_p(3, 5, 4)
+    arrive_p(0, 1, 7)
+    arrive_q(0)
+    tiles((0, 1, 7), (0,))
+    arrive_q(1, 2, 6)
+    tiles((0, 1, 7), (1, 2, 6))
+    arrive_p(2, 6, 3, 5, 4)
     arrive_q(3, 7, 4, 5)
 
     joined = jnp.where(lane1 < 4, qbuf[0, 12:13], -1.0)
@@ -254,7 +243,7 @@
     pair_copy = p_copy(s1buf.at[0], s1buf, s1_recv, 1, 4)
     pair_copy.start()
     pair_copy.wait_recv()
-    s2buf[0] = s1buf[0] + s1buf[1]
+    s2buf[0:1] = s1buf[0] + s1buf[1]
 
     xs = [lax.rem(x + d, NX) * NZ for d in range(NX)]
     ys = [lax.rem(y + d, NY) * NC + core for d in range(NY)]
@@ -266,13 +255,13 @@
 
     for slot in sorted(range(1, CHIPS), key=hops, reverse=True):
         pltpu.make_async_remote_copy(
-            src_ref=s2buf.at[0], dst_ref=s2buf.at[slot],
+            src_ref=s2buf.at[pl.ds(0, 1)], dst_ref=s2buf.at[pl.ds(slot, 1)],
             send_sem=send_sem.at[5, 0], recv_sem=s2_recv.at[0],
             device_id=(xs[slot // 32] + zs[slot % 8], ys[slot // 8 % 4]), device_id_type=MESH,
         ).start()
     rest = s2buf.at[pl.ds(1, CHIPS - 1)]
     pltpu.make_async_copy(rest, rest, s2_recv.at[0]).wait()
-    total = jnp.sum(s2buf[...], axis=0)
+    total = jnp.sum(s2buf[...], axis=0, keepdims=True)
     sums = jnp.sum(jnp.where(sub16 == lane16, total, 0.0), axis=1, keepdims=True)
     rr, curv, ri, ii = (sums[4 * i : 4 * i + 4] for i in range(4))
     alpha = rr / curv
@@ -292,9 +281,10 @@
 def local(points, length_scales, noise, tile_table, solution, residual, direction):
     hbm = pl.BlockSpec(memory_space=pltpu.HBM)
     dma = pltpu.SemaphoreType.DMA
+    arrays = (length_scales, noise.reshape(1), tile_table, points, solution, residual, direction)
     out = pl.pallas_call(
         body,
-        out_shape=jax.ShapeDtypeStruct((12, W), F32),
+        out_shape=pltpu.VMEM((12, W), F32),
         in_specs=[hbm] * 7,
         out_specs=pl.BlockSpec(memory_space=pltpu.VMEM),
         scratch_shapes=[
@@ -310,7 +300,7 @@
             pltpu.VMEM((GROUP, 1, W), F32),
             pltpu.VMEM((GROUP, 16, W), F32),
             pltpu.VMEM((2, 1, W), F32),
-            pltpu.VMEM((CHIPS, 1, W), F32),
+            pltpu.VMEM((CHIPS, W), F32),
             pltpu.VMEM((GROUP, 16, W), F32),
             pltpu.VMEM((GROUP * W, DEPTH), BF16),
             pltpu.VMEM((DEPTH, GROUP * W), BF16),
@@ -321,9 +311,9 @@
         + [dma((GROUP,))] * 6
         + [dma((6, GROUP))],
         compiler_params=pltpu.CompilerParams(
-            collective_id=0, has_side_effects=True, vmem_limit_bytes=64 * 2**20 - 65536
+            collective_id=0, has_side_effects=True, vmem_limit_bytes=40 * 2**20
         ),
-    )(length_scales, noise.reshape(1), tile_table, points, solution, residual, direction)
+    )(*(a if i in (1,) else pltpu.with_memory_space_constraint(a, pltpu.HBM) for i, a in enumerate(arrays)))
     return out[0:4], out[4:8], out[8:12]
 
 

time: 41.3 us -> 38.9 us (0.942)
  Pallas kernels: 38.6 us -> 36.9 us
  local copies, waits for them, and re-layouts: 1.34 us -> 0.59 us
    pallas_call x1, Pallas kernels: 38.6 us -> 36.9 us  [local(): pl.pallas_call(body, out_shape=pltpu.VMEM((12, W), F32), in_specs=[hbm] *...]
    slice x1, local copies, waits for them, and re-layouts: 1.34 us -> 0.59 us  [local(): return (out[0:4], out[4:8], out[8:12])]
where the time goes in v3:
time: 38.9 us; the launch traced here: 38.8 us
  Pallas kernels  36.9 us (95%)
  between operations  1.29 us (3%)
  local copies, waits for them, and re-layouts  0.59 us (2%)
    pallas_call x1, Pallas kernels, local(): pl.pallas_call(body, out_shape=pltpu.VMEM((12, W), F32), in_specs=[hbm] *...  36.9 us

profile of v3, /device:TPU:1, one launch (start us, length us, event | category | flops | bytes accessed | tf_op | source)
XLA Modules:
  0.0 38.8 jit_solution(7777035520308780123)
XLA Ops:
  1.3 36.9 %shard_map.94 = f32[12,128]{1,0:T(8,128)S(1)} custom-call(f32[8]{0:T(128)} %scales_in.1, f32[1]{0:T(128)} %bitcast.1.noise_in, s32[4]{0:T(128)} %table_in.1, f32[8,128]{1,0:T(8,128)} %points_in.1, f32[4,128]{1,0:T(4,128)} %sol_in.1, f32[4,128]{1,0:T(4,128)} %res_in.1, f32[4,128]{1,0:T(4,128)} %dirs_in.1), custom_call_target="tpu_custom_call" | custom-call | tf_op jit(solution)/shard_map/pallas_call | solution.py:285
  38.2 0.6 %fusion = (f32[4,128]{1,0:T(4,128)}, f32[4,128]{1,0:T(4,128)}, f32[4,128]{1,0:T(4,128)}) fusion(f32[12,128]{1,0:T(8,128)S(1)} %shard_map.94), kind=kLoop, calls=%fused_computation | loop fusion | bytes 12288 | tf_op jit(solution)/shard_map/slice | solution.py:317

commit v4 on v3

--- a/solution.py
+++ b/solution.py
@@ -55,7 +55,7 @@
 def body(
     scales_in, noise_in, table_in, points_in, sol_in, res_in, dirs_in, out,
     scales, noise, table, points, sol, res, dirs,
-    pbuf, qbuf, tbuf, rbuf, s1buf, s2buf, sendr, left, right, dlhs, acc,
+    pbuf, qbuf, tbuf, rbuf, s1buf, s2buf, sendr, left, right, dlhs, acc, weights,
     in_sem, p_recv, q_recv, t_recv, r_recv, s1_recv, s2_recv, send_sem,
 ):
     row, col = lax.axis_index("row"), lax.axis_index("col")
@@ -82,10 +82,12 @@
         )
     ]
     others = range(1, GROUP)
+    far_p = (8, 9, 6, 7, 10, 11, 4, 5, 12, 13, 2, 3, 14, 15, 1)
+    far_q = (10, 9, 11, 6, 14, 2, 8, 5, 7, 13, 15, 1, 3, 4, 12)
     barrier = pltpu.get_barrier_semaphore()
-    for k in others:
+    for k, m in zip(far_p, far_q):
         pl.semaphore_signal(barrier, inc=1, device_id=p_at(k, 1), device_id_type=MESH)
-        pl.semaphore_signal(barrier, inc=1, device_id=q_at(k, 1), device_id_type=MESH)
+        pl.semaphore_signal(barrier, inc=1, device_id=q_at(m, 1), device_id_type=MESH)
 
     for load in loads:
         load.start()
@@ -121,15 +123,15 @@
     pl.semaphore_wait(barrier, 2 * (GROUP - 1))
     p_copies = {k: p_copy(pbuf.at[0], pbuf, p_recv, k, 0) for k in others}
     q_copies = {k: q_copy(qbuf.at[0], qbuf, q_recv, k, 1) for k in others}
-    for k in others:
+    for k, m in zip(far_p, far_q):
         p_copies[k].start()
-        q_copies[k].start()
+        q_copies[m].start()
 
     def prep_right(k):
         right[:, pl.ds(k * W, W)] = right_rows(pbuf[k]).astype(BF16)
 
     def prep_left(m):
-        left[pl.ds(m * W, W), :] = left_rows(qbuf[m, 0:8]).T.astype(BF16)
+        left[pl.ds(m * W, W), :] = left_rows(qbuf[m, 0:8]).astype(BF16).T
         h, mid, low = split3(qbuf[m, 8:12])
         dlhs[:, pl.ds(m * W, W)] = jnp.concatenate([h, mid, low, jnp.zeros_like(h)], 0).astype(BF16)
 
@@ -172,21 +174,13 @@
                     tile(pair, pair // 2, first, ppair)
                     done.add((ppair, pair))
 
-    arrive_p(0, 1, 7)
+    arrive_p(1, 7)
     arrive_q(0)
-    tiles((0, 1, 7), (0,))
+    tiles((1, 7), (0,))
     arrive_q(1, 2, 6)
-    tiles((0, 1, 7), (1, 2, 6))
-    arrive_p(2, 6, 3, 5, 4)
+    tiles((1, 7), (1, 2, 6))
+    arrive_p(4, 3, 5, 2, 6, 0)
     arrive_q(3, 7, 4, 5)
-
-    joined = jnp.where(lane1 < 4, qbuf[0, 12:13], -1.0)
-    for m in others:
-        joined = jnp.where(lax.div(lane1, 4) == m, qbuf[m, 12:13], joined)
-    tbuf[0] = joined
-    t_copies = {k: p_copy(tbuf.at[0], tbuf, t_recv, k, 2) for k in others}
-    for k in others:
-        t_copies[k].start()
 
     r_copies = {k: p_copy(sendr.at[k], rbuf, r_recv, k, 3, -1) for k in others}
     def finish(ppairs):
@@ -200,9 +194,17 @@
             if k > 0:
                 r_copies[k].start()
 
-    region(lambda: finish((4, 3, 5)))
-    region(lambda: finish((2, 6)))
-    region(lambda: finish((1, 7, 0)))
+    finish((4,))
+    joined = jnp.where(lane1 < 4, qbuf[0, 12:13], -1.0)
+    for m in others:
+        joined = jnp.where(lax.div(lane1, 4) == m, qbuf[m, 12:13], joined)
+    tbuf[0] = joined
+    t_copies = {k: p_copy(tbuf.at[0], tbuf, t_recv, k, 2) for k in others}
+    for k in far_p:
+        t_copies[k].start()
+
+    for ppair in (3, 5, 6, 2, 1):
+        finish((ppair,))
 
     for k in others:
         t_copies[k].wait_recv()
@@ -218,9 +220,7 @@
     )
     degree = jnp.sum(jnp.sum(degree, axis=1, keepdims=True), axis=0, keepdims=True)
     mine = [jnp.where(lane1 < 16, t[0:1], -1.0) for t in tt]
-    d = dirs[...]
-    weighted = jnp.zeros((16, W), F32)
-    for kz in (4, 3, 5, 2, 6, 1, 7, 0):
+    for kz in range(NZ):
         at = (NZ - kz) % NZ
         block = (lax.rem(x + NX - group, NX) * NZ + lax.rem(z + kz, NZ)).astype(F32)
         linked = jnp.where(lax.div(lane16, 16) == group, lists_me[at : at + 1], 0.0)
@@ -228,10 +228,19 @@
         weight = jnp.sum(linked, axis=1, keepdims=True)
         if kz == 0:
             weight = jnp.where(sub16[:, 0:1] < 4, 1.0 + degree, weight)
+        weights[kz] = jnp.broadcast_to(weight, (16, W))
+
+    for ppair in (7, 0):
+        finish((ppair,))
+
+
+    d = dirs[...]
+    weighted = jnp.zeros((16, W), F32)
+    for kz in (4, 3, 5, 2, 6, 1, 7, 0):
         for k in (2 * kz, 2 * kz + 1):
             if k > 0:
                 r_copies[k].wait_recv()
-            weighted += weight * (rbuf[k] if k > 0 else sendr[0])
+            weighted += weights[kz] * (rbuf[k] if k > 0 else sendr[0])
     image = sum(weighted[4 * mx : 4 * mx + 4] for mx in range(NX)) + noise[0] * d
 
     loads[5].wait()
@@ -306,6 +315,7 @@
             pltpu.VMEM((DEPTH, GROUP * W), BF16),
             pltpu.VMEM((16, GROUP * W), BF16),
             pltpu.VMEM((NX, 16, GROUP * W), F32),
+            pltpu.VMEM((NZ, 16, W), F32),
             dma((7,)),
         ]
         + [dma((GROUP,))] * 6

time: 38.9 us -> 38.7 us (level)
  no operation moved by 1% of the time
where the time goes in v4:
time: 38.7 us; the launch traced here: 38.5 us
  Pallas kernels  36.7 us (95%)
  between operations  1.29 us (3%)
  local copies, waits for them, and re-layouts  0.59 us (2%)
    pallas_call x1, Pallas kernels, local(): pl.pallas_call(body, out_shape=pltpu.VMEM((12, W), F32), in_specs=[hbm] *...  36.7 us

profile of v4, /device:TPU:1, one launch (start us, length us, event | category | flops | bytes accessed | tf_op | source)
XLA Modules:
  0.0 38.5 jit_solution(510775070964122332)
XLA Ops:
  1.3 36.7 %shard_map.94 = f32[12,128]{1,0:T(8,128)S(1)} custom-call(f32[8]{0:T(128)} %scales_in.1, f32[1]{0:T(128)} %bitcast.1.noise_in, s32[4]{0:T(128)} %table_in.1, f32[8,128]{1,0:T(8,128)} %points_in.1, f32[4,128]{1,0:T(4,128)} %sol_in.1, f32[4,128]{1,0:T(4,128)} %res_in.1, f32[4,128]{1,0:T(4,128)} %dirs_in.1), custom_call_target="tpu_custom_call" | custom-call | tf_op jit(solution)/shard_map/pallas_call | solution.py:294
  37.9 0.6 %fusion = (f32[4,128]{1,0:T(4,128)}, f32[4,128]{1,0:T(4,128)}, f32[4,128]{1,0:T(4,128)}) fusion(f32[12,128]{1,0:T(8,128)S(1)} %shard_map.94), kind=kLoop, calls=%fused_computation | loop fusion | bytes 12288 | tf_op jit(solution)/shard_map/slice | solution.py:327

commit v5 on v4

--- a/solution.py
+++ b/solution.py
@@ -14,6 +14,8 @@
 POINT_SCALE = math.sqrt(5.0 / 3.0)
 NX, NY, NZ, NC = 4, 4, 8, 2
 CHIPS = NX * NY * NZ
+P_GROUPS = ((1, 1), (2, 3), (14, 15), (4, 13))
+Q_GROUPS = ((1, 1), (2, 5), (12, 13), (6, 11), (14, 15))
 GROUP = 16
 W = 128
 DEPTH = 64
@@ -108,15 +110,28 @@
     qbuf[0, 8:12] = dirs[...]
     qbuf[0, 12:16] = jnp.broadcast_to(own_table, (4, W))
 
+    groups = {id(p_recv): P_GROUPS, id(q_recv): Q_GROUPS}
+
+    def group_of(recv, k):
+        spans = groups.get(id(recv), ((1, 15),))
+        return [i for i, (first, last) in enumerate(spans) if first <= k <= last][0]
+
+    def wait_bytes(ref, sem):
+        pltpu.make_async_copy(ref, ref, sem).wait()
+
+    def arrive(buf, recv, group):
+        first, last = groups.get(id(recv), ((1, 15),))[group]
+        wait_bytes(buf.at[pl.ds(first, last - first + 1)], recv.at[group])
+
     def p_copy(src, buf, recv, k, sem, sign=1):
         return pltpu.make_async_remote_copy(
-            src_ref=src, dst_ref=buf.at[k], send_sem=send_sem.at[sem, k], recv_sem=recv.at[k],
+            src_ref=src, dst_ref=buf.at[k], send_sem=send_sem.at[sem], recv_sem=recv.at[group_of(recv, k)],
             device_id=p_at(k, sign), device_id_type=MESH,
         )
 
     def q_copy(src, buf, recv, k, sem):
         return pltpu.make_async_remote_copy(
-            src_ref=src, dst_ref=buf.at[k], send_sem=send_sem.at[sem, k], recv_sem=recv.at[k],
+            src_ref=src, dst_ref=buf.at[k], send_sem=send_sem.at[sem], recv_sem=recv.at[group_of(recv, k)],
             device_id=q_at(k, 1), device_id_type=MESH,
         )
 
@@ -147,18 +162,14 @@
         at = (mx, slice(None), pl.ds(p0, 256))
         acc[at] = both if first else acc[at] + both
 
-    def arrive_p(*pairs):
+    def take_p(*pairs):
         for pair in pairs:
             for k in (2 * pair, 2 * pair + 1):
-                if k > 0:
-                    p_copies[k].wait_recv()
                 prep_right(k)
 
-    def arrive_q(*pairs):
+    def take_q(*pairs):
         for pair in pairs:
             for m in (2 * pair, 2 * pair + 1):
-                if m > 0:
-                    q_copies[m].wait_recv()
                 prep_left(m)
 
     def region(step):
@@ -174,13 +185,22 @@
                     tile(pair, pair // 2, first, ppair)
                     done.add((ppair, pair))
 
-    arrive_p(1, 7)
-    arrive_q(0)
+    arrive(pbuf, p_recv, 1)
+    arrive(pbuf, p_recv, 2)
+    take_p(1, 7)
+    arrive(qbuf, q_recv, 0)
+    take_q(0)
     tiles((1, 7), (0,))
-    arrive_q(1, 2, 6)
+    arrive(qbuf, q_recv, 1)
+    arrive(qbuf, q_recv, 2)
+    take_q(1, 2, 6)
     tiles((1, 7), (1, 2, 6))
-    arrive_p(4, 3, 5, 2, 6, 0)
-    arrive_q(3, 7, 4, 5)
+    arrive(pbuf, p_recv, 0)
+    arrive(pbuf, p_recv, 3)
+    take_p(4, 3, 5, 2, 6, 0)
+    arrive(qbuf, q_recv, 3)
+    arrive(qbuf, q_recv, 4)
+    take_q(3, 7, 4, 5)
 
     r_copies = {k: p_copy(sendr.at[k], rbuf, r_recv, k, 3, -1) for k in others}
     def finish(ppairs):
@@ -206,8 +226,7 @@
     for ppair in (3, 5, 6, 2, 1):
         finish((ppair,))
 
-    for k in others:
-        t_copies[k].wait_recv()
+    arrive(tbuf, t_recv, 0)
 
     sub16 = lax.broadcasted_iota(jnp.int32, (16, W), 0)
     lane16 = lax.broadcasted_iota(jnp.int32, (16, W), 1)
@@ -235,11 +254,10 @@
 
 
     d = dirs[...]
+    arrive(rbuf, r_recv, 0)
     weighted = jnp.zeros((16, W), F32)
     for kz in (4, 3, 5, 2, 6, 1, 7, 0):
         for k in (2 * kz, 2 * kz + 1):
-            if k > 0:
-                r_copies[k].wait_recv()
             weighted += weights[kz] * (rbuf[k] if k > 0 else sendr[0])
     image = sum(weighted[4 * mx : 4 * mx + 4] for mx in range(NX)) + noise[0] * d
 
@@ -265,11 +283,15 @@
     for slot in sorted(range(1, CHIPS), key=hops, reverse=True):
         pltpu.make_async_remote_copy(
             src_ref=s2buf.at[pl.ds(0, 1)], dst_ref=s2buf.at[pl.ds(slot, 1)],
-            send_sem=send_sem.at[5, 0], recv_sem=s2_recv.at[0],
+            send_sem=send_sem.at[5], recv_sem=s2_recv.at[0],
             device_id=(xs[slot // 32] + zs[slot % 8], ys[slot // 8 % 4]), device_id_type=MESH,
         ).start()
     rest = s2buf.at[pl.ds(1, CHIPS - 1)]
-    pltpu.make_async_copy(rest, rest, s2_recv.at[0]).wait()
+    pair_copy.wait_send()
+    for phase, buf in enumerate((pbuf, qbuf, tbuf, rbuf)):
+        wait_bytes(buf.at[pl.ds(1, GROUP - 1)], send_sem.at[phase])
+    wait_bytes(rest, send_sem.at[5])
+    wait_bytes(rest, s2_recv.at[0])
     total = jnp.sum(s2buf[...], axis=0, keepdims=True)
     sums = jnp.sum(jnp.where(sub16 == lane16, total, 0.0), axis=1, keepdims=True)
     rr, curv, ri, ii = (sums[4 * i : 4 * i + 4] for i in range(4))
@@ -280,11 +302,6 @@
     out[0:4] = sol[...] + alpha * d
     out[4:8] = nr
     out[8:12] = nr + beta * d
-    pair_copy.wait_send()
-    pltpu.make_async_copy(rest, rest, send_sem.at[5, 0]).wait()
-    for copies in (p_copies, q_copies, t_copies, r_copies):
-        for k in others:
-            copies[k].wait_send()
 
 
 def local(points, length_scales, noise, tile_table, solution, residual, direction):
@@ -319,7 +336,7 @@
             dma((7,)),
         ]
         + [dma((GROUP,))] * 6
-        + [dma((6, GROUP))],
+        + [dma((6,))],
         compiler_params=pltpu.CompilerParams(
             collective_id=0, has_side_effects=True, vmem_limit_bytes=40 * 2**20
         ),

time: 38.7 us -> 36.8 us (0.951)
  Pallas kernels: 36.7 us -> 34.8 us
    pallas_call x1, Pallas kernels: 36.7 us -> 34.8 us  [local(): pl.pallas_call(body, out_shape=pltpu.VMEM((12, W), F32), in_specs=[hbm] *...]
where the time goes in v5:
time: 36.8 us; the launch traced here: 36.7 us
  Pallas kernels  34.8 us (95%)
  between operations  1.29 us (4%)
  local copies, waits for them, and re-layouts  0.59 us (2%)
    pallas_call x1, Pallas kernels, local(): pl.pallas_call(body, out_shape=pltpu.VMEM((12, W), F32), in_specs=[hbm] *...  34.8 us

profile of v5, /device:TPU:1, one launch (start us, length us, event | category | flops | bytes accessed | tf_op | source)
XLA Modules:
  0.0 36.7 jit_solution(14822533424265209469)
XLA Ops:
  1.3 34.8 %shard_map.94 = f32[12,128]{1,0:T(8,128)S(1)} custom-call(f32[8]{0:T(128)} %scales_in.1, f32[1]{0:T(128)} %bitcast.1.noise_in, s32[4]{0:T(128)} %table_in.1, f32[8,128]{1,0:T(8,128)} %points_in.1, f32[4,128]{1,0:T(4,128)} %sol_in.1, f32[4,128]{1,0:T(4,128)} %res_in.1, f32[4,128]{1,0:T(4,128)} %dirs_in.1), custom_call_target="tpu_custom_call" | custom-call | tf_op jit(solution)/shard_map/pallas_call | solution.py:311
  36.1 0.6 %fusion = (f32[4,128]{1,0:T(4,128)}, f32[4,128]{1,0:T(4,128)}, f32[4,128]{1,0:T(4,128)}) fusion(f32[12,128]{1,0:T(8,128)S(1)} %shard_map.94), kind=kLoop, calls=%fused_computation | loop fusion | bytes 12288 | tf_op jit(solution)/shard_map/slice | solution.py:344

commit v6 on v5

--- a/solution.py
+++ b/solution.py
@@ -28,24 +28,27 @@
     return high, mid, rest - mid
 
 
-def norm_rows(a, first):
-    n = split3(jnp.sum(a * a, axis=0, keepdims=True))
-    row = lax.broadcasted_iota(jnp.int32, a.shape, 0)
-    at = 0 if first else 3
-    ones = ((row >= 3 - at) & (row < 6 - at)).astype(F32)
-    for k in range(3):
-        ones = jnp.where(row == at + k, n[k], ones)
-    return ones
+def rows_of(values):
+    row = lax.broadcasted_iota(jnp.int32, (8, W), 0)
+    out = jnp.zeros((8, W), F32)
+    for k, value in values.items():
+        out = jnp.where(row == k, value, out)
+    return out
+
+
+def split_norm(a):
+    return split3(jnp.sum(a * a, axis=0, keepdims=True))
 
 
 def right_rows(a):
     h, m, l = split3(a)
-    return jnp.concatenate([h, h, h, m, m, l, norm_rows(a, False), jnp.zeros_like(a)], 0)
-
-
-def left_rows(a):
+    norm = rows_of(dict(enumerate(split_norm(a))))
+    return jnp.concatenate([h, h, h, m, m, l, rows_of({4: 1.0, 5: 1.0, 6: 1.0}), norm], 0)
+
+
+def left_rows(a, half):
     h, m, l = (-2.0 * part for part in split3(a))
-    return jnp.concatenate([h, m, l, h, m, h, norm_rows(a, True), jnp.zeros_like(a)], 0)
+    return jnp.concatenate([h, m, l, h, m, h, half, rows_of({0: 1.0, 1: 1.0, 2: 1.0})], 0)
 
 
 def kern_of(s):
@@ -108,7 +111,9 @@
         own_table = jnp.where(lax.rem(lane1, 4) == s, table[s].astype(F32), own_table)
     qbuf[0, 0:8] = a
     qbuf[0, 8:12] = dirs[...]
-    qbuf[0, 12:16] = jnp.broadcast_to(own_table, (4, W))
+    for k, part in enumerate(split_norm(a)):
+        qbuf[0, 12 + k : 13 + k] = part
+    qbuf[0, 15:16] = own_table
 
     groups = {id(p_recv): P_GROUPS, id(q_recv): Q_GROUPS}
 
@@ -146,19 +151,25 @@
         right[:, pl.ds(k * W, W)] = right_rows(pbuf[k]).astype(BF16)
 
     def prep_left(m):
-        left[pl.ds(m * W, W), :] = left_rows(qbuf[m, 0:8]).astype(BF16).T
+        left[pl.ds(m * W, W), :] = left_rows(qbuf[m, 0:8], qbuf[m, 8:16]).astype(BF16).T
         h, mid, low = split3(qbuf[m, 8:12])
         dlhs[:, pl.ds(m * W, W)] = jnp.concatenate([h, mid, low, jnp.zeros_like(h)], 0).astype(BF16)
 
     def tile(pair, mx, first, ppair):
-        q0, p0 = pair * 256, ppair * 256
-        s = jnp.dot(left[pl.ds(q0, 256), :], right[:, pl.ds(p0, 256)], preferred_element_type=F32)
-        kern = kern_of(s)
-        high = kern.astype(BF16)
-        low = (kern - high.astype(F32)).astype(BF16)
-        d = dlhs[:, pl.ds(q0, 256)]
-        both = jnp.dot(d, high, preferred_element_type=F32)
-        both += jnp.dot(d, low, preferred_element_type=F32)
+        add_tiles((pair,), mx, first, ppair)
+
+    def add_tiles(pairs, mx, first, ppair):
+        p0 = ppair * 256
+        both = None
+        for q0 in (pair * 256 for pair in pairs):
+            s = jnp.dot(left[pl.ds(q0, 256), :], right[:, pl.ds(p0, 256)], preferred_element_type=F32)
+            kern = kern_of(s)
+            high = kern.astype(BF16)
+            low = (kern - high.astype(F32)).astype(BF16)
+            d = dlhs[:, pl.ds(q0, 256)]
+            part = jnp.dot(d, high, preferred_element_type=F32)
+            part += jnp.dot(d, low, preferred_element_type=F32)
+            both = part if both is None else both + part
         at = (mx, slice(None), pl.ds(p0, 256))
         acc[at] = both if first else acc[at] + both
 
@@ -180,6 +191,9 @@
     def tiles(ppairs, pairs):
         for ppair in ppairs:
             for pair in pairs:
+                if pair % 2 == 0 and pair + 1 in pairs and not {(ppair, pair), (ppair, pair + 1)} & done:
+                    add_tiles((pair, pair + 1), pair // 2, True, ppair)
+                    done.update({(ppair, pair), (ppair, pair + 1)})
                 if (ppair, pair) not in done:
                     first = (ppair, pair ^ 1) not in done
                     tile(pair, pair // 2, first, ppair)
@@ -215,15 +229,18 @@
                 r_copies[k].start()
 
     finish((4,))
-    joined = jnp.where(lane1 < 4, qbuf[0, 12:13], -1.0)
+    joined = jnp.where(lane1 < 4, qbuf[0, 15:16], -1.0)
     for m in others:
-        joined = jnp.where(lax.div(lane1, 4) == m, qbuf[m, 12:13], joined)
+        joined = jnp.where(lax.div(lane1, 4) == m, qbuf[m, 15:16], joined)
     tbuf[0] = joined
     t_copies = {k: p_copy(tbuf.at[0], tbuf, t_recv, k, 2) for k in others}
     for k in far_p:
         t_copies[k].start()
 
     for ppair in (3, 5, 6, 2, 1):
+        finish((ppair,))
+
+    for ppair in (7, 0):
         finish((ppair,))
 
     arrive(tbuf, t_recv, 0)
@@ -248,9 +265,6 @@
         if kz == 0:
             weight = jnp.where(sub16[:, 0:1] < 4, 1.0 + degree, weight)
         weights[kz] = jnp.broadcast_to(weight, (16, W))
-
-    for ppair in (7, 0):
-        finish((ppair,))
 
 
     d = dirs[...]

time: 36.8 us -> 36.7 us (level)
  no operation moved by 1% of the time
where the time goes in v6:
time: 36.7 us; the launch traced here: 36.5 us
  Pallas kernels  34.7 us (95%)
  between operations  1.29 us (4%)
  local copies, waits for them, and re-layouts  0.59 us (2%)
    pallas_call x1, Pallas kernels, local(): pl.pallas_call(body, out_shape=pltpu.VMEM((12, W), F32), in_specs=[hbm] *...  34.7 us

profile of v6, /device:TPU:1, one launch (start us, length us, event | category | flops | bytes accessed | tf_op | source)
XLA Modules:
  0.0 36.5 jit_solution(11127431137268867182)
XLA Ops:
  1.3 34.7 %shard_map.94 = f32[12,128]{1,0:T(8,128)S(1)} custom-call(f32[8]{0:T(128)} %scales_in.1, f32[1]{0:T(128)} %bitcast.1.noise_in, s32[4]{0:T(128)} %table_in.1, f32[8,128]{1,0:T(8,128)} %points_in.1, f32[4,128]{1,0:T(4,128)} %sol_in.1, f32[4,128]{1,0:T(4,128)} %res_in.1, f32[4,128]{1,0:T(4,128)} %dirs_in.1), custom_call_target="tpu_custom_call" | custom-call | tf_op jit(solution)/shard_map/pallas_call | solution.py:325
  36.0 0.6 %fusion = (f32[4,128]{1,0:T(4,128)}, f32[4,128]{1,0:T(4,128)}, f32[4,128]{1,0:T(4,128)}) fusion(f32[12,128]{1,0:T(8,128)S(1)} %shard_map.94), kind=kLoop, calls=%fused_computation | loop fusion | bytes 12288 | tf_op jit(solution)/shard_map/slice | solution.py:358
